TPU v7x, 512 devices: a whole 4x8x8 slice. The times are simulated.
512 devices in a mesh: occ: 16 (over y, core), vir: 32 (over x, z).
Axes of the slice: x: 4, y: 8, z: 8, core: 2. Of those that a mesh axis runs over, the one named last changes fastest.
Arguments:
- amplitudes: float32 [2048, 12288], P('occ', 'vir'), may hold values from -6 to 6
- integrals: float32 [12288, 4096], P('vir', 'occ'), may hold values from -0.109375 to 0.109375
- pair_mask: int32 [32, 192], P('occ', 'vir'), may hold values 0 or 1
- tile_mask: int32 [192, 64], P('vir', 'occ'), may hold values 0 or 1
Outputs:
- residual: float32 [2048, 4096], P('occ', 'vir')
Inputs may be any that keep to these rules, and one draw needn't show every extreme that they name: `pair_mask`: 0 marks a tile that is absent and contributes nothing. `tile_mask`: 0 marks a tile that is absent and contributes nothing.
All inputs are finite; a program needn't handle non-finite values. No bound on the sum of `pair_mask` or of `tile_mask` on one device may be relied on, other than what follows from the above.
Results may differ from a plain program's by a relative error of at most 0.00007.
Values sent between devices are 32-bit elements; how exact they have to be, the bound alone decides.
No kernel may reach another device: no remote copies, remote signals or barrier semaphores. Data moves between devices by JAX's collectives and lax.ppermute only.
A program may use at most 64 MiB of HBM per device.

v0:
```python
import jax
import jax.numpy as jnp
from jax import lax
from jax.sharding import PartitionSpec as P


def expand(mask, width):
    grown = jnp.repeat(mask.astype(jnp.float32), width, axis=0)
    return jnp.repeat(grown, width, axis=1)


def body(amplitudes, integrals, pair_mask, tile_mask):
    tile_width = amplitudes.shape[1] // pair_mask.shape[1]
    masked_t = amplitudes * expand(pair_mask, tile_width)
    masked_v = integrals * expand(tile_mask, tile_width)
    partial_sum = jnp.dot(
        masked_t,
        lax.all_gather(masked_v, "occ", axis=1, tiled=True),
        precision=lax.Precision.HIGHEST,
        preferred_element_type=jnp.float32,
    )
    return lax.psum_scatter(partial_sum, "vir", scatter_dimension=1, tiled=True)


def solution(mesh):
    in_specs = (P("occ", "vir"), P("vir", "occ"), P("occ", "vir"), P("vir", "occ"))
    out_specs = P("occ", "vir")
    return jax.shard_map(body, mesh=mesh, in_specs=in_specs, out_specs=out_specs, check_vma=False)
```

profile of v0, /device:TPU:8, one launch (start us, length us, event | category | flops | bytes accessed | tf_op | source)
XLA Modules:
  0.0 302.7 jit_solution(3729471157549326904)
XLA Ops:
  6.5 0.0 all-gather.2.cloned.1.call-start
  6.5 0.7 convert_element_type.7
  7.2 0.1 broadcast_in_dim.14
  7.3 0.1 reshape.14
  7.4 1.2 copy.11
  8.5 0.8 bitcast_multiply_fusion
  9.3 0.0 all-gather.2.cloned.1.call-update
  9.3 0.0 reduce-scatter.2.cloned.1.call-start
  9.4 0.7 convert_element_type.6
  10.1 0.1 copy.9
  10.2 0.1 broadcast_in_dim.12
  10.2 0.1 reshape.12
  10.3 1.1 copy.10
  11.4 51.0 %all-gather.2.cloned.1.call-done = f32[384,4096]{0,1:T(8,128)} async-done(((f32[384,256]{0,1:T(8,128)}), f32[384,4096]{0,1:T(8,128)}) %all-gather.2.cloned.1.call-update) | async-done | bytes 6291472 | tf_op jit(solution)/shard_map/all_gather | solution.py:18
  62.4 10.7 %fusion = f32[128,4096]{1,0:T(8,128)} fusion(f32[128,384]{0,1:T(8,128)S(1)} %bitcast_multiply_fusion.1, f32[384,4096]{0,1:T(8,128)} %all-gather.2.cloned.1.call-done), kind=kOutput, calls=%fused_computation.2 | convolution fusion | flops 2415919104 | bytes 8585216 | tf_op jit(solution)/shard_map/dot_general | solution.py:16
  73.0 0.0 reduce-scatter.2.cloned.1.call-update
  73.1 222.8 %reduce-scatter.2.cloned.1.call-done = f32[128,128]{1,0:T(8,128)} async-done(((f32[128,4096]{1,0:T(8,128)}), f32[128,128]{1,0:T(8,128)}) %reduce-scatter.2.cloned.1.call-update) | async-done | bytes 65552 | tf_op jit(solution)/shard_map/reduce_scatter | solution.py:22
  (1 shorter events, 0.0 us)
Async XLA Ops:
  6.5 55.9 %all-gather.2.cloned.1.call-start = ((), (), s32[]{:S(2)}) async-start(), calls=%async_computation.1 | async-start | bytes 6684672 | tf_op jit(solution)/shard_map/all_gather | solution.py:18
  9.3 286.5 %reduce-scatter.2.cloned.1.call-start = ((), (), s32[]{:S(2)}) async-start(), calls=%async_computation.2 | async-start | bytes 2162688 | tf_op jit(solution)/shard_map/reduce_scatter | solution.py:22
Sparse Core Ops, SparseCore 0:
  9.5 52.8 all-gather.1
  73.2 222.6 reduce-scatter.1
where the time goes:
time: 303 us
  waiting for transfers between devices  274 us (90%)
  between operations  13.4 us (4%)
  matrix products  10.7 us (4%)
    reduce_scatter x1, waiting for transfers between devices, body(): return lax.psum_scatter(partial_sum, 'vir', scatter_dimension=1, tiled=True)  223 us
    all_gather x1, waiting for transfers between devices, body(): lax.all_gather(masked_v, 'occ', axis=1, tiled=True)  51 us
    dot_general x1, matrix products, body(): jnp.dot(masked_t, lax.all_gather(masked_v, 'occ', axis=1, tiled=True), pr...  10.7 us
  transfers between devices with their start and end apart: 2, of which 2 were waited for; matrix products, arithmetic and copies ran while one was open for 1% of the time, Pallas kernels for 0%

commit v1 on v0

--- a/solution.py
+++ b/solution.py
@@ -2,6 +2,19 @@
 import jax.numpy as jnp
 from jax import lax
 from jax.sharding import PartitionSpec as P
+
+
+def gather_around(x, axis, dim):
+    ways = lax.axis_size(axis)
+    up = [(d, (d + 1) % ways) for d in range(ways)]
+    down = [(d, (d - 1) % ways) for d in range(ways)]
+    earlier, later = ([x], [x])
+    for _ in range(ways // 2):
+        earlier.append(lax.ppermute(earlier[-1], axis, up))
+    for _ in range((ways - 1) // 2):
+        later.append(lax.ppermute(later[-1], axis, down))
+    line = jnp.concatenate([*earlier[::-1], *later[1:]], axis=dim)
+    return jnp.roll(line, (lax.axis_index(axis) - ways // 2) * x.shape[dim], axis=dim)
 
 
 def expand(mask, width):
@@ -15,7 +28,7 @@
     masked_v = integrals * expand(tile_mask, tile_width)
     partial_sum = jnp.dot(
         masked_t,
-        lax.all_gather(masked_v, "occ", axis=1, tiled=True),
+        gather_around(masked_v, "occ", 1),
         precision=lax.Precision.HIGHEST,
         preferred_element_type=jnp.float32,
     )

time: 303 us -> 331 us (1.092)
  starting transfers between devices: 0.04 us -> 18.4 us
  local copies, waits for them, and re-layouts: 2.62 us -> 14.2 us
    all_gather x1 -> x0, waiting for transfers between devices: 51 us -> none  [body(): lax.all_gather(masked_v, 'occ', axis=1, tiled=True)]
    ppermute x0 -> x15, waiting for transfers between devices: none -> 41.4 us  [the longest x8 41.4 us: gather_around(): earlier.append(lax.ppermute(earlier[-1], axis, up))]
    ppermute x0 -> x15, starting transfers between devices: none -> 18.4 us  [the longest x7 18.4 us: gather_around(): later.append(lax.ppermute(later[-1], axis, down))]
    unnamed x2 -> x41, local copies, waits for them, and re-layouts: 2.21 us -> 13.7 us
    reduce_scatter x1, waiting for transfers between devices: 223 us -> 232 us  [body(): return lax.psum_scatter(partial_sum, 'vir', scatter_dimension=1, tiled=True)]
  transfers between devices with their start and end apart: 2 -> 16, of which waited for: 2 -> 9; matrix products, arithmetic and copies ran while one was open for 1% -> 3% of each run, Pallas kernels for 0% -> 0%
where the time goes in v1:
time: 331 us; the launch traced here: 330 us
  waiting for transfers between devices  274 us (83%)
  starting transfers between devices  18.4 us (6%)
  local copies, waits for them, and re-layouts  14.2 us (4%)
  between operations  13.7 us (4%)
  matrix products  7.81 us (2%)
    reduce_scatter x1, waiting for transfers between devices, body(): return lax.psum_scatter(partial_sum, 'vir', scatter_dimension=1, tiled=True)  232 us
    ppermute x8, waiting for transfers between devices, gather_around(): earlier.append(lax.ppermute(earlier[-1], axis, up))  41.4 us
    ppermute x7, starting transfers between devices, gather_around(): later.append(lax.ppermute(later[-1], axis, down))  18.4 us
    unnamed x41, local copies, waits for them, and re-layouts  13.7 us
    dot_general x1, matrix products, body(): jnp.dot(masked_t, gather_around(masked_v, 'occ', 1), precision=lax.Precis...  7.81 us
  transfers between devices with their start and end apart: 16, of which 9 were waited for; matrix products, arithmetic and copies ran while one was open for 3% of the time, Pallas kernels for 0%

profile of v1, /device:TPU:8, one launch (start us, length us, event | category | flops | bytes accessed | tf_op | source)
XLA Modules:
  0.0 330.2 jit_solution(14224820483853003224)
XLA Ops:
  6.5 0.0 reduce-scatter.2.cloned.1.call-start
  6.5 1.2 copy.11
  7.7 0.7 convert_element_type.7
  8.4 0.1 broadcast_in_dim.14
  8.5 0.1 reshape.14
  8.6 0.0 collective-permute-start
  8.6 7.2 %collective-permute-done = f32[384,256]{0,1:T(8,128)S(1)} collective-permute-done((f32[384,256]{0,1:T(8,128)S(1)}, f32[384,256]{0,1:T(8,128)S(1)}, u32[]{:S(2)}, u32[]{:S(2)}) %collective-permute-start) | collective-permute-done | bytes 393248 | tf_op jit(solution)/shard_map/ppermute | solution.py:13
  15.8 0.0 collective-permute-start.1
  15.8 1.7 collective-permute-start.8
  17.5 5.5 %collective-permute-done.1 = f32[384,256]{0,1:T(8,128)S(1)} collective-permute-done((f32[384,256]{0,1:T(8,128)S(1)}, f32[384,256]{0,1:T(8,128)S(1)}, u32[]{:S(2)}, u32[]{:S(2)}) %collective-permute-start.1) | collective-permute-done | bytes 393248 | tf_op jit(solution)/shard_map/ppermute | solution.py:13
  23.0 0.0 collective-permute-start.2
  23.0 0.0 collective-permute-done.8
  23.0 1.7 collective-permute-start.9
  24.7 5.5 %collective-permute-done.2 = f32[384,256]{0,1:T(8,128)S(1)} collective-permute-done((f32[384,256]{0,1:T(8,128)S(1)}, f32[384,256]{0,1:T(8,128)S(1)}, u32[]{:S(2)}, u32[]{:S(2)}) %collective-permute-start.2) | collective-permute-done | bytes 393248 | tf_op jit(solution)/shard_map/ppermute | solution.py:13
  30.2 0.0 collective-permute-start.3
  30.2 0.0 collective-permute-done.9
  30.2 2.5 collective-permute-start.10
  32.7 5.3 %collective-permute-done.3 = f32[384,256]{0,1:T(8,128)S(1)} collective-permute-done((f32[384,256]{0,1:T(8,128)S(1)}, f32[384,256]{0,1:T(8,128)S(1)}, u32[]{:S(2)}, u32[]{:S(2)}) %collective-permute-start.3) | collective-permute-done | bytes 393248 | tf_op jit(solution)/shard_map/ppermute | solution.py:13
  38.0 0.0 collective-permute-start.4
  38.0 0.0 collective-permute-done.10
  38.0 3.1 collective-permute-start.11
  41.1 5.3 %collective-permute-done.4 = f32[384,256]{0,1:T(8,128)S(1)} collective-permute-done((f32[384,256]{0,1:T(8,128)S(1)}, f32[384,256]{0,1:T(8,128)S(1)}, u32[]{:S(2)}, u32[]{:S(2)}) %collective-permute-start.4) | collective-permute-done | bytes 393248 | tf_op jit(solution)/shard_map/ppermute | solution.py:13
  46.4 0.0 copy-start
  46.4 0.0 collective-permute-start.5
  46.5 0.0 collective-permute-done.11
  46.5 3.1 collective-permute-start.12
  49.5 5.3 %collective-permute-done.5 = f32[384,256]{0,1:T(8,128)S(1)} collective-permute-done((f32[384,256]{0,1:T(8,128)S(1)}, f32[384,256]{0,1:T(8,128)S(1)}, u32[]{:S(2)}, u32[]{:S(2)}) %collective-permute-start.5) | collective-permute-done | bytes 393248 | tf_op jit(solution)/shard_map/ppermute | solution.py:13
  54.9 0.0 copy-start.2
  54.9 0.0 collective-permute-start.6
  54.9 0.0 collective-permute-done.12
  54.9 0.0 copy-done
  54.9 3.2 collective-permute-start.13
  58.1 0.0 copy-done.2
  58.1 5.3 %collective-permute-done.6 = f32[384,256]{0,1:T(8,128)} collective-permute-done((f32[384,256]{0,1:T(8,128)S(1)}, f32[384,256]{0,1:T(8,128)}, u32[]{:S(2)}, u32[]{:S(2)}) %collective-permute-start.6) | collective-permute-done | bytes 393248 | tf_op jit(solution)/shard_map/ppermute | solution.py:13
  63.4 0.0 collective-permute-start.7
  63.4 1.7 copy.10
  65.1 0.7 convert_element_type.6
  65.8 0.1 copy.9
  65.9 0.1 broadcast_in_dim.12
  66.0 0.1 reshape.12
  66.1 0.0 copy-start.3
  66.1 0.0 copy-start.1
  66.1 1.0 bitcast_multiply_fusion.1
  67.1 0.0 collective-permute-done.13
  67.1 3.0 collective-permute-start.14
  70.1 2.1 collective-permute-done.7
  72.1 1.0 constant_dynamic-update-slice_fusion.31
  73.2 1.0 constant_dynamic-update-slice_fusion.30
  74.2 1.0 constant_dynamic-update-slice_fusion.29
  75.2 1.0 constant_dynamic-update-slice_fusion.28
  76.6 1.0 constant_dynamic-update-slice_fusion.18
  77.6 1.0 constant_dynamic-update-slice_fusion.17
  78.6 0.0 collective-permute-done.14
  78.7 1.0 constant_dynamic-update-slice_fusion.15
  79.7 1.0 constant_dynamic-update-slice_fusion.14
  80.7 0.0 copy-done.3
  80.8 0.0 copy-done.1
  81.1 1.0 constant_dynamic-update-slice_fusion.2
  82.2 1.0 constant_dynamic-update-slice_fusion.1
  83.2 7.8 %fusion = f32[128,4096]{1,0:T(8,128)} fusion(f32[128,384]{0,1:T(8,128)S(1)} %bitcast_multiply_fusion.1, f32[384,8192]{0,1:T(8,128)S(1)} %constant_dynamic-update-slice_fusion, s32[]{:T(128)S(6)} %select_n.14), kind=kOutput, calls=%fused_computation | convolution fusion | flops 2415919104 | bytes 8585220 | tf_op jit(solution)/shard_map/dot_general | solution.py:29
  91.0 0.0 reduce-scatter.2.cloned.1.call-update
  91.1 232.3 %reduce-scatter.2.cloned.1.call-done = f32[128,128]{1,0:T(8,128)} async-done(((f32[128,4096]{1,0:T(8,128)}), f32[128,128]{1,0:T(8,128)}) %reduce-scatter.2.cloned.1.call-update) | async-done | bytes 65552 | tf_op jit(solution)/shard_map/reduce_scatter | solution.py:35
  (23 shorter events, 0.7 us)
Async XLA Ops:
  6.5 316.9 %reduce-scatter.2.cloned.1.call-start = ((), (), s32[]{:S(2)}) async-start(), calls=%async_computation.1 | async-start | bytes 2162688 | tf_op jit(solution)/shard_map/reduce_scatter | solution.py:35
  8.6 7.2 %collective-permute-start = (f32[384,256]{0,1:T(8,128)S(1)}, f32[384,256]{0,1:T(8,128)S(1)}, u32[]{:S(2)}, u32[]{:S(2)}) collective-permute-start(f32[384,256]{0,1:T(8,128)S(1)} %bitcast_multiply_fusion), channel_id=1, source_target_pairs={{0,32},{32,64},{64,96},{96,128},{128,160},{160,192},{192,224},{224... | collective-permute-start | bytes 1179656 | tf_op jit(solution)/shard_map/ppermute | solution.py:13
  15.8 7.2 %collective-permute-start.1 = (f32[384,256]{0,1:T(8,128)S(1)}, f32[384,256]{0,1:T(8,128)S(1)}, u32[]{:S(2)}, u32[]{:S(2)}) collective-permute-start(f32[384,256]{0,1:T(8,128)S(1)} %collective-permute-done), channel_id=1, source_target_pairs={{0,32},{32,64},{64,96},{96,128},{128,160},{160,192},{192,224},{224... | collective-permute-start | bytes 1179656 | tf_op jit(solution)/shard_map/ppermute | solution.py:13
  15.8 7.2 %collective-permute-start.8 = (f32[384,256]{0,1:T(8,128)S(1)}, f32[384,256]{0,1:T(8,128)S(1)}, u32[]{:S(2)}, u32[]{:S(2)}) collective-permute-start(f32[384,256]{0,1:T(8,128)S(1)} %bitcast_multiply_fusion), channel_id=1, source_target_pairs={{0,480},{32,0},{64,32},{96,64},{128,96},{160,128},{192,160},{224,1... | collective-permute-start | bytes 1179656 | tf_op jit(solution)/shard_map/ppermute | solution.py:15
  23.0 7.2 %collective-permute-start.2 = (f32[384,256]{0,1:T(8,128)S(1)}, f32[384,256]{0,1:T(8,128)S(1)}, u32[]{:S(2)}, u32[]{:S(2)}) collective-permute-start(f32[384,256]{0,1:T(8,128)S(1)} %collective-permute-done.1), channel_id=1, source_target_pairs={{0,32},{32,64},{64,96},{96,128},{128,160},{160,192},{192,224},{224... | collective-permute-start | bytes 1179656 | tf_op jit(solution)/shard_map/ppermute | solution.py:13
  23.0 7.2 %collective-permute-start.9 = (f32[384,256]{0,1:T(8,128)S(1)}, f32[384,256]{0,1:T(8,128)S(1)}, u32[]{:S(2)}, u32[]{:S(2)}) collective-permute-start(f32[384,256]{0,1:T(8,128)S(1)} %collective-permute-done.8), channel_id=1, source_target_pairs={{0,480},{32,0},{64,32},{96,64},{128,96},{160,128},{192,160},{224,1... | collective-permute-start | bytes 1179656 | tf_op jit(solution)/shard_map/ppermute | solution.py:15
  30.2 7.8 %collective-permute-start.3 = (f32[384,256]{0,1:T(8,128)S(1)}, f32[384,256]{0,1:T(8,128)S(1)}, u32[]{:S(2)}, u32[]{:S(2)}) collective-permute-start(f32[384,256]{0,1:T(8,128)S(1)} %collective-permute-done.2), channel_id=1, source_target_pairs={{0,32},{32,64},{64,96},{96,128},{128,160},{160,192},{192,224},{224... | collective-permute-start | bytes 1179656 | tf_op jit(solution)/shard_map/ppermute | solution.py:13
  30.2 7.8 %collective-permute-start.10 = (f32[384,256]{0,1:T(8,128)S(1)}, f32[384,256]{0,1:T(8,128)S(1)}, u32[]{:S(2)}, u32[]{:S(2)}) collective-permute-start(f32[384,256]{0,1:T(8,128)S(1)} %collective-permute-done.9), channel_id=1, source_target_pairs={{0,480},{32,0},{64,32},{96,64},{128,96},{160,128},{192,160},{224,1... | collective-permute-start | bytes 1179656 | tf_op jit(solution)/shard_map/ppermute | solution.py:15
  38.0 8.4 %collective-permute-start.4 = (f32[384,256]{0,1:T(8,128)S(1)}, f32[384,256]{0,1:T(8,128)S(1)}, u32[]{:S(2)}, u32[]{:S(2)}) collective-permute-start(f32[384,256]{0,1:T(8,128)S(1)} %collective-permute-done.3), channel_id=1, source_target_pairs={{0,32},{32,64},{64,96},{96,128},{128,160},{160,192},{192,224},{224... | collective-permute-start | bytes 1179656 | tf_op jit(solution)/shard_map/ppermute | solution.py:13
  38.0 8.4 %collective-permute-start.11 = (f32[384,256]{0,1:T(8,128)S(1)}, f32[384,256]{0,1:T(8,128)S(1)}, u32[]{:S(2)}, u32[]{:S(2)}) collective-permute-start(f32[384,256]{0,1:T(8,128)S(1)} %collective-permute-done.10), channel_id=1, source_target_pairs={{0,480},{32,0},{64,32},{96,64},{128,96},{160,128},{192,160},{224,1... | collective-permute-start | bytes 1179656 | tf_op jit(solution)/shard_map/ppermute | solution.py:15
  46.4 8.4 %copy-start = (f32[384,256]{0,1:T(8,128)}, f32[384,256]{0,1:T(8,128)S(1)}, u32[]{:S(2)}) copy-start(f32[384,256]{0,1:T(8,128)S(1)} %collective-permute-done.4) | copy-start | bytes 1179652
  46.4 8.4 %collective-permute-start.5 = (f32[384,256]{0,1:T(8,128)S(1)}, f32[384,256]{0,1:T(8,128)S(1)}, u32[]{:S(2)}, u32[]{:S(2)}) collective-permute-start(f32[384,256]{0,1:T(8,128)S(1)} %collective-permute-done.4), channel_id=1, source_target_pairs={{0,32},{32,64},{64,96},{96,128},{128,160},{160,192},{192,224},{224... | collective-permute-start | bytes 1179656 | tf_op jit(solution)/shard_map/ppermute | solution.py:13
  46.5 8.4 %collective-permute-start.12 = (f32[384,256]{0,1:T(8,128)S(1)}, f32[384,256]{0,1:T(8,128)}, u32[]{:S(2)}, u32[]{:S(2)}) collective-permute-start(f32[384,256]{0,1:T(8,128)S(1)} %collective-permute-done.11), channel_id=1, source_target_pairs={{0,480},{32,0},{64,32},{96,64},{128,96},{160,128},{192,160},{224,1... | collective-permute-start | bytes 1179656 | tf_op jit(solution)/shard_map/ppermute | solution.py:15
  54.9 3.2 copy-start.2
  54.9 8.5 %collective-permute-start.6 = (f32[384,256]{0,1:T(8,128)S(1)}, f32[384,256]{0,1:T(8,128)}, u32[]{:S(2)}, u32[]{:S(2)}) collective-permute-start(f32[384,256]{0,1:T(8,128)S(1)} %collective-permute-done.5), channel_id=1, source_target_pairs={{0,32},{32,64},{64,96},{96,128},{128,160},{160,192},{192,224},{224... | collective-permute-start | bytes 1179656 | tf_op jit(solution)/shard_map/ppermute | solution.py:13
  54.9 12.2 %collective-permute-start.13 = (f32[384,256]{0,1:T(8,128)}, f32[384,256]{0,1:T(8,128)}, u32[]{:S(2)}, u32[]{:S(2)}) collective-permute-start(f32[384,256]{0,1:T(8,128)} %collective-permute-done.12), channel_id=1, source_target_pairs={{0,480},{32,0},{64,32},{96,64},{128,96},{160,128},{192,160},{224,1... | collective-permute-start | bytes 1179656 | tf_op jit(solution)/shard_map/ppermute | solution.py:15
  63.4 8.8 %collective-permute-start.7 = (f32[384,256]{0,1:T(8,128)}, f32[384,256]{0,1:T(8,128)}, u32[]{:S(2)}, u32[]{:S(2)}) collective-permute-start(f32[384,256]{0,1:T(8,128)} %collective-permute-done.6), channel_id=1, source_target_pairs={{0,32},{32,64},{64,96},{96,128},{128,160},{160,192},{192,224},{224... | collective-permute-start | bytes 1179656 | tf_op jit(solution)/shard_map/ppermute | solution.py:13
  66.1 14.7 %copy-start.3 = (f32[384,256]{0,1:T(8,128)S(1)}, f32[384,256]{0,1:T(8,128)}, u32[]{:S(2)}) copy-start(f32[384,256]{0,1:T(8,128)} %copy-done.2) | copy-start | bytes 1179652
  66.1 14.7 %copy-start.1 = (f32[384,256]{0,1:T(8,128)S(1)}, f32[384,256]{0,1:T(8,128)}, u32[]{:S(2)}) copy-start(f32[384,256]{0,1:T(8,128)} %copy-done) | copy-start | bytes 1179652
  67.1 11.5 %collective-permute-start.14 = (f32[384,256]{0,1:T(8,128)}, f32[384,256]{0,1:T(8,128)S(1)}, u32[]{:S(2)}, u32[]{:S(2)}) collective-permute-start(f32[384,256]{0,1:T(8,128)} %collective-permute-done.13), channel_id=1, source_target_pairs={{0,480},{32,0},{64,32},{96,64},{128,96},{160,128},{192,160},{224,1... | collective-permute-start | bytes 1179656 | tf_op jit(solution)/shard_map/ppermute | solution.py:15
Sparse Core Ops, SparseCore 0:
  91.2 232.1 reduce-scatter.1
